TPU v7x, 32 devices: a whole 2x2x4 slice. The times are simulated.
32 devices in a mesh: groups: 2 (over x), dp: 16 (over z, y, core).
Axes of the slice: x: 2, y: 2, z: 4, core: 2. Of those that a mesh axis runs over, the one named last changes fastest.
Arguments:
- features: bfloat16 [32768, 128], P(('groups', 'dp')), parts along dimension 0, may hold values from -6 to 6
- treatment: int32 [32768], P(('groups', 'dp')), parts along dimension 0, may hold values 0 or 1
- outcome: int32 [32768], P(('groups', 'dp')), parts along dimension 0, may hold values 0 or 1
- head: bfloat16 [2, 512], replicated, may hold values from -0.25 to 0.25
- positions: float32 [8, 128, 512], P('groups'), parts along dimension 0, may hold values from -0.5 to 0.5
- momenta: float32 [8, 128, 512], P('groups'), parts along dimension 0, may hold values from -1.8 to 1.8
- inverse_temps: float32 [8], P('groups'), parts along dimension 0, may hold values from 0.1 to 1
- step_sizes: float32 [8], P('groups'), parts along dimension 0, may hold values from 0.05 to 0.15
- accept: int32 [6], P('groups'), parts along dimension 0, may hold values 0 or 1
Outputs:
- new_positions: float32 [8, 128, 512], P('groups'), parts along dimension 0
- new_momenta: float32 [8, 128, 512], P('groups'), parts along dimension 0
- mean_nll: float32 [8], P('groups'), parts along dimension 0
There are 2 independent parts, one for each index of `groups`. A program takes and returns all parts, laid end to end along the dimension named above; an argument that names none is the same for every part. Nothing has to cross between parts.
All inputs are finite; a program needn't handle non-finite values. No bound on the sum of `treatment` or of `outcome` on one device may be relied on, other than what follows from the above.
Results may differ from a plain program's by a relative error of at most 0.013.
Values may be sent and summed in bfloat16 or wider, within the bound.
A program may use at most 64 MiB of HBM per device.

v0:
```python
import jax
import jax.numpy as jnp
from jax import lax
from jax.sharding import PartitionSpec as P

LEAPS = 4


def evaluate(features, treatment, outcome, head, weights_bf):
    pre = jnp.einsum("nf,rfh->rnh", features, weights_bf, preferred_element_type=jnp.float32)
    hidden = jnp.tanh(pre)
    head_f = head.astype(jnp.float32)
    coef = head_f[0][None, :] + treatment.astype(jnp.float32)[:, None] * head_f[1][None, :]
    logit = jnp.sum(hidden * coef[None], axis=2)
    target = outcome.astype(jnp.float32)[None, :]
    nll = jnp.sum(jax.nn.softplus(logit) - target * logit, axis=1)
    resid = jax.nn.sigmoid(logit) - target
    delta = (resid[:, :, None] * coef[None] * (1.0 - hidden * hidden)).astype(jnp.bfloat16)
    grad = jnp.einsum("nf,rnh->rfh", features, delta, preferred_element_type=jnp.float32)
    return (grad, nll)


def rung_order(accept, rungs):
    order = jnp.arange(rungs, dtype=jnp.int32)
    for k in range(rungs - 1):
        taken = accept[k] == 1
        lower = order[k]
        upper = order[k + 1]
        order = order.at[k].set(jnp.where(taken, upper, lower))
        order = order.at[k + 1].set(jnp.where(taken, lower, upper))
    return order


def summed_whole(grad, nll):
    return lax.psum((grad, nll), "dp")


def local(
    features, treatment, outcome, head, positions, momenta, inverse_temps, step_sizes, accept
):
    rungs = positions.shape[0]
    total_rows = features.shape[0] * lax.axis_size("dp")
    beta = inverse_temps[:, None, None]
    eps = step_sizes[:, None, None]
    order = rung_order(accept, rungs)
    theta = positions
    moment = momenta
    grad, nll = evaluate(features, treatment, outcome, head, theta.astype(jnp.bfloat16))
    grad, loss = summed_whole(grad, nll)
    force = beta * grad + theta
    for leap in range(LEAPS):
        moment = moment - 0.5 * eps * force
        theta = theta + eps * moment
        grad, nll = evaluate(features, treatment, outcome, head, theta.astype(jnp.bfloat16))
        grad, loss = summed_whole(grad, nll)
        force = beta * grad + theta
        moment = moment - 0.5 * eps * force
    mean_rung = loss / total_rows
    return (
        jnp.take(theta, order, axis=0),
        jnp.take(moment, order, axis=0),
        jnp.take(mean_rung, order, axis=0),
    )


def solution(mesh):
    placed = (
        P(("groups", "dp"), None),
        P(("groups", "dp")),
        P(("groups", "dp")),
        P(),
        P("groups", None, None),
        P("groups", None, None),
        P("groups"),
        P("groups"),
        P("groups"),
    )
    return jax.shard_map(
        local,
        mesh=mesh,
        in_specs=placed,
        out_specs=(P("groups", None, None), P("groups", None, None), P("groups")),
        check_vma=False,
    )
```

profile of v0, /device:TPU:0, one launch (start us, length us, event | category | flops | bytes accessed | tf_op | source)
XLA Modules:
  0.0 527.2 jit_solution(2178910583926168464)
XLA Ops:
  9.6 2.7 fusion.16
  12.4 3.0 fusion.42
  15.4 1.3 copy.21
  16.8 2.5 copy.20
  19.3 92.1 %all-reduce.6.cloned.1.call-done = f32[4,128,512]{1,2,0:T(8,128)} async-done(((f32[4,128,512]{1,2,0:T(8,128)}), f32[4,128,512]{1,2,0:T(8,128)}) %all-reduce.6.cloned.1.call-update) | async-done | bytes 1048592 | tf_op jit(solution)/shard_map/psum | solution.py:35
  111.4 2.1 multiply_add_fusion.4
  113.5 1.3 fusion.12
  114.9 2.9 fusion.39
  117.9 92.7 %all-reduce.8.cloned.1.call-done = f32[4,128,512]{1,2,0:T(8,128)} async-done(((f32[4,128,512]{1,2,0:T(8,128)}), f32[4,128,512]{1,2,0:T(8,128)}) %all-reduce.8.cloned.1.call-update) | async-done | bytes 1048592 | tf_op jit(solution)/shard_map/psum | solution.py:35
  210.5 2.5 subtract_subtract_fusion.2
  214.0 1.4 fusion.8
  215.4 2.9 fusion.36
  219.9 91.2 %all-reduce.10.cloned.1.call-done = f32[4,128,512]{1,2,0:T(8,128)} async-done(((f32[4,128,512]{1,2,0:T(8,128)}), f32[4,128,512]{1,2,0:T(8,128)}) %all-reduce.10.cloned.1.call-update) | async-done | bytes 1048592 | tf_op jit(solution)/shard_map/psum | solution.py:35
  311.0 2.9 fusion.4
  314.0 2.9 fusion.33
  320.5 89.2 %all-reduce.12.cloned.1.call-done = f32[4,128,512]{1,2,0:T(8,128)} async-done(((f32[4,128,512]{1,2,0:T(8,128)}), f32[4,128,512]{1,2,0:T(8,128)}) %all-reduce.12.cloned.1.call-update) | async-done | bytes 1048592 | tf_op jit(solution)/shard_map/psum | solution.py:35
  409.6 3.5 multiply_add_fusion.1
  414.1 1.3 fusion
  415.6 3.0 fusion.30
  418.6 30.8 %psum.47 = f32[4]{0:T(128)S(1)} all-reduce(f32[4]{0:T(128)S(1)} %get-tuple-element.87), channel_id=1, replica_groups=mesh['groups'=2,'dp'=16] {'dp'}, use_global_device_ids=true, to_apply=%region_11.0 | all-reduce | flops 4 | bytes 32 | tf_op jit(solution)/shard_map/psum | solution.py:35
  451.1 59.9 %all-reduce.14.cloned.1.call-done = f32[4,128,512]{1,2,0:T(8,128)} async-done(((f32[4,128,512]{1,2,0:T(8,128)}), f32[4,128,512]{1,2,0:T(8,128)}) %all-reduce.14.cloned.1.call-update) | async-done | bytes 1048592 | tf_op jit(solution)/shard_map/psum | solution.py:35
  511.1 2.7 multiply_subtract_fusion
  513.8 1.8 gather_fusion.2
  516.8 2.5 copy.22
  (53 shorter events, 14.1 us)
Async XLA Ops:
  7.2 2.5 copy-start
  7.2 104.2 %all-reduce.6.cloned.1.call-start = ((), (), s32[]{:S(2)}) async-start(), calls=%async_computation | async-start | bytes 2097152 | tf_op jit(solution)/shard_map/psum | solution.py:35
  12.3 3.1 copy-start.4
  12.4 6.9 %copy-start.6 = (f32[4]{0:T(128)S(1)}, f32[4]{0:T(128)}, u32[]{:S(2)}) copy-start(f32[4]{0:T(128)} %param.30) | copy-start | bytes 52
  12.4 99.0 %copy-start.5 = (f32[4]{0:T(128)S(1)}, f32[4]{0:T(128)}, u32[]{:S(2)}) copy-start(f32[4]{0:T(128)} %param.29) | copy-start | bytes 52
  15.4 195.1 %all-reduce.8.cloned.1.call-start = ((), (), s32[]{:S(2)}) async-start(), calls=%async_computation.1 | async-start | bytes 2097152 | tf_op jit(solution)/shard_map/psum | solution.py:35
  117.8 193.2 %all-reduce.10.cloned.1.call-start = ((), (), s32[]{:S(2)}) async-start(), calls=%async_computation.2 | async-start | bytes 2097152 | tf_op jit(solution)/shard_map/psum | solution.py:35
  213.1 1.0 copy-start.3
  215.4 3.2 copy-start.7
  218.4 191.3 %all-reduce.12.cloned.1.call-start = ((), (), s32[]{:S(2)}) async-start(), calls=%async_computation.3 | async-start | bytes 2097152 | tf_op jit(solution)/shard_map/psum | solution.py:35
  316.9 194.2 %all-reduce.14.cloned.1.call-start = ((), (), s32[]{:S(2)}) async-start(), calls=%async_computation.4 | async-start | bytes 2097152 | tf_op jit(solution)/shard_map/psum | solution.py:35
  413.1 1.0 copy-start.1
  415.4 34.0 %copy-start.2 = (f32[4,128,512]{1,2,0:T(8,128)S(1)}, f32[4,128,512]{1,2,0:T(8,128)}, u32[]{:S(2)}) copy-start(f32[4,128,512]{1,2,0:T(8,128)} %copy-done.1) | copy-start | bytes 3145732
Sparse Core Ops, SparseCore 0:
  15.5 95.8 all-reduce.5
  117.9 92.5 all-reduce.7
  218.5 92.5 all-reduce.9
  317.0 92.5 all-reduce.11
  418.7 92.3 all-reduce.13
where the time goes:
time: 528 us; the launch traced here: 527 us
  waiting for transfers between devices  425 us (80%)
  blocking collectives  30.8 us (6%)
  matrix products  24.2 us (5%)
  other arithmetic  17.9 us (3%)
  local copies, waits for them, and re-layouts  14.8 us (3%)
  between operations  14 us (3%)
    psum x5, waiting for transfers between devices, summed_whole(): return lax.psum((grad, nll), 'dp')  425 us
    psum x1, blocking collectives, summed_whole(): return lax.psum((grad, nll), 'dp')  30.8 us
    dot_general x5, matrix products, evaluate(): jnp.einsum('nf,rnh->rfh', features, delta, preferred_element_type=jnp.flo...  14.6 us
  transfers between devices with their start and end apart: 5, of which 5 were waited for; matrix products, arithmetic and copies ran while one was open for 2% of the time, Pallas kernels for 0%

commit v1 on v0

v1 whole, which is shorter than its diff:
```python
import functools
import jax
import jax.numpy as jnp
from jax import lax
from jax.experimental import pallas as pl
from jax.experimental.pallas import tpu as pltpu
from jax.sharding import PartitionSpec as P

LEAPS = 4
LOCAL = 2
MESH = pl.DeviceIdType.MESH
F32 = jnp.float32
BF16 = jnp.bfloat16


def chain_kernel(
    line,
    block,
    feat_ref,
    treat_ref,
    outcome_ref,
    head_ref,
    pos_ref,
    mom_ref,
    temp_ref,
    step_ref,
    th_ref,
    mo_ref,
    loss_ref,
    load_buf,
    xt,
    ty,
    coef,
    base_b,
    effect_b,
    slope,
    pre_buf,
    near_left,
    line_left,
    full_left,
    gsum,
    near_send,
    near_recv,
    line_send,
    line_recv,
    gfull,
    loss_own,
    loss_near,
    loss_line,
    load_sem,
    in_sem,
    near_sem,
    line_sem,
    aline_sem,
    anear_sem,
    lnear_sem,
    lline_sem,
    out_sem,
):
    group = lax.axis_index("groups")
    me = lax.axis_index("dp")
    core = lax.rem(me, 2)
    near = lax.rem(me // 2, 2)
    far = me // 4
    rows = feat_ref.shape[0]
    hidden = head_ref.shape[1]
    half = hidden // 2
    shard = half // line
    items = LOCAL * (LEAPS + 1)

    def device(z, y, c):
        return (group, (z * 2 + y) * 2 + c)

    core_peer = device(far, near, 1 - core)
    near_peer = device(far, 1 - near, core)
    line_peers = [lax.rem(far + d, line) for d in range(1, line)]

    def remote(src, dst, sems, where):
        return pltpu.make_async_remote_copy(
            src_ref=src,
            dst_ref=dst,
            send_sem=sems[0],
            recv_sem=sems[1],
            device_id=where,
            device_id_type=MESH,
        )

    loads = []
    for s in range(LOCAL):
        for a, src in enumerate((pos_ref, mom_ref)):
            loads.append(
                pltpu.make_async_copy(
                    src.at[core * LOCAL + s], load_buf.at[2 * s + a], load_sem.at[2 * s + a]
                )
            )
    for copy in loads:
        copy.start()

    barrier = pltpu.get_barrier_semaphore()
    pl.semaphore_signal(barrier, inc=1, device_id=core_peer, device_id_type=MESH)
    pl.semaphore_signal(barrier, inc=1, device_id=near_peer, device_id_type=MESH)
    for z in line_peers:
        pl.semaphore_signal(
            barrier, inc=1, device_id=device(z, near, core), device_id_type=MESH
        )

    xt[0] = feat_ref[...].T
    ty[0, 0:1] = treat_ref[...].astype(F32)
    ty[0, 1:2] = outcome_ref[...].astype(F32)
    ty[0, 2:8] = jnp.zeros((6, rows), F32)
    pl.semaphore_wait(barrier, line + 1)
    copy_x = remote(xt.at[0], xt.at[1], (in_sem.at[0], in_sem.at[1]), core_peer)
    copy_t = remote(ty.at[0], ty.at[1], (in_sem.at[2], in_sem.at[3]), core_peer)
    copy_x.start()
    copy_t.start()

    loss_own[...] = jnp.zeros_like(loss_own)
    near_left[...] = jnp.zeros_like(near_left)
    line_left[...] = jnp.zeros_like(line_left)
    full_left[...] = jnp.zeros_like(full_left)
    head = head_ref[...].astype(F32)
    base_b[...] = jnp.broadcast_to(head[0:1], (128, hidden)).T
    effect_b[...] = jnp.broadcast_to(head[1:2], (128, hidden)).T
    for s in range(LOCAL):
        loads[2 * s].wait()
        th_ref[core * LOCAL + s] = load_buf[2 * s].T
        loads[2 * s + 1].wait()
        mo_ref[core * LOCAL + s] = load_buf[2 * s + 1].T
    copy_t.wait()
    for part in range(2):
        for g in range(rows // 128):
            span = slice(g * 128, (g + 1) * 128)
            coef[part, :, span] = base_b[...] + ty[part, 0:1, span] * effect_b[...]
    copy_x.wait()

    def near_reduce(slot):
        return remote(
            near_send.at[slot],
            near_recv.at[slot],
            (near_sem.at[slot, 0], near_sem.at[slot, 1]),
            near_peer,
        )

    def line_reduce(slot, d):
        z = line_peers[d]
        return remote(
            line_send.at[slot, pl.ds(pl.multiple_of(z * shard, shard), shard)],
            line_recv.at[slot, d],
            (line_sem.at[slot, d, 0], line_sem.at[slot, d, 1]),
            device(z, near, core),
        )

    def line_gather(slot, d):
        mine = pl.ds(pl.multiple_of(near * half + far * shard, shard), shard)
        return remote(
            gfull.at[slot, mine],
            gfull.at[slot, mine],
            (aline_sem.at[slot, d, 0], aline_sem.at[slot, d, 1]),
            device(line_peers[d], near, core),
        )

    def near_gather(slot):
        mine = pl.ds(pl.multiple_of(near * half, half), half)
        return remote(
            gfull.at[slot, mine],
            gfull.at[slot, mine],
            (anear_sem.at[slot, 0], anear_sem.at[slot, 1]),
            near_peer,
        )

    def loss_to_near():
        return remote(loss_own, loss_near, (lnear_sem.at[0], lnear_sem.at[1]), near_peer)

    def loss_to_line(d):
        return remote(
            loss_line.at[far],
            loss_line.at[far],
            (lline_sem.at[d, 0], lline_sem.at[d, 1]),
            device(line_peers[d], near, core),
        )

    def loss_to_core():
        mine = pl.ds(pl.multiple_of(core * 8, 8), 8)
        return remote(
            loss_ref.at[mine], loss_ref.at[mine], (out_sem.at[2, 0, 0], out_sem.at[2, 0, 1]), core_peer
        )

    def result_to_core(ref, a, slot):
        rung = core * LOCAL + slot
        return remote(
            ref.at[rung], ref.at[rung], (out_sem.at[a, slot, 0], out_sem.at[a, slot, 1]), core_peer
        )

    def carry_weight(k):
        leap = k // LOCAL
        return jnp.where(leap == 1, 0.5, jnp.where(leap == LEAPS, 2.0, 1.0)).astype(F32)

    def rounded(value, left, slot, k):
        value = value + carry_weight(k) * left[slot]
        sent = value.astype(BF16)
        left[slot] = value - sent.astype(F32)
        return sent

    def evaluate(slot, part):
        weights = th_ref[core * LOCAL + slot].astype(BF16)
        total = jnp.zeros((1, 128), F32)
        step = 64
        for b in range(rows // block):
            span = slice(b * block, (b + 1) * block)
            pre = pre_buf.at[b % 2]
            pre[...] = jnp.dot(weights, xt[part, :, span], preferred_element_type=F32)
            acc = jnp.zeros((8, block), F32)
            for j in range(0, hidden, step):
                act = jnp.tanh(pre[j : j + step])
                scale = coef[part, j : j + step, span]
                term = act * scale
                acc = acc + jnp.sum(term.reshape(step // 8, 8, block), axis=0)
                pre[j : j + step] = scale - act * term
            logit = jnp.sum(acc, axis=0, keepdims=True)
            target = ty[part, 1:2, span]
            small = jnp.exp(-jnp.abs(logit))
            nll = jnp.maximum(logit, 0.0) + jnp.log(1.0 + small) - target * logit
            resid = jnp.where(logit >= 0.0, 1.0, small) / (1.0 + small) - target
            for j in range(0, hidden, step):
                slope[j : j + step, span] = (pre[j : j + step] * resid).astype(BF16)
            for g in range(block // 128):
                total = total + nll[:, g * 128 : (g + 1) * 128]
        grad = lax.dot_general(
            slope[...], xt[part], (((1,), (1,)), ((), ())), preferred_element_type=F32
        )
        row = lax.broadcasted_iota(jnp.int32, (8, 128), 0)
        total = jnp.broadcast_to(total, (8, 128))
        if part == 0:
            gsum[slot] = grad
            loss_own[...] = jnp.where(row == slot, total, loss_own[...])
        else:
            gsum[slot] = gsum[slot] + grad
            loss_own[...] = jnp.where(row == slot, total + loss_own[...], loss_own[...])

    def send_near(k, slot):
        other = pl.ds(pl.multiple_of((1 - near) * half, half), half)
        near_send[slot] = rounded(gsum[slot, other], near_left, slot, k)
        near_reduce(slot).start()

        @pl.when(k == items - 1)
        def _():
            loss_to_near().start()

    def reduced_near(k, slot):
        near_reduce(slot).wait()
        mine = pl.ds(pl.multiple_of(near * half, half), half)
        summed = gsum[slot, mine] + near_recv[slot].astype(F32)
        gsum[slot, mine] = summed
        line_send[slot] = rounded(summed, line_left, slot, k)
        for d in range(line - 1):
            line_reduce(slot, d).start()

        @pl.when(k == items - 1)
        def _():
            loss_to_near().wait()
            loss_line[far] = loss_own[...] + loss_near[...]
            for d in range(line - 1):
                loss_to_line(d).start()

    def reduced_line(k, slot):
        mine = pl.ds(pl.multiple_of(near * half + far * shard, shard), shard)
        summed = gsum[slot, mine]
        for d in range(line - 1):
            line_reduce(slot, d).wait()
            summed = summed + line_recv[slot, d].astype(F32)
        gfull[slot, mine] = rounded(summed, full_left, slot, k)
        for d in range(line - 1):
            line_gather(slot, d).start()

        @pl.when(k == items - 1)
        def _():
            for d in range(line - 1):
                loss_to_line(d).wait()
            whole = loss_line[0]
            for z in range(1, line):
                whole = whole + loss_line[z]
            loss_ref[pl.ds(pl.multiple_of(core * 8, 8), 8)] = whole
            loss_to_core().start()

    def gathered_line(slot):
        for d in range(line - 1):
            line_gather(slot, d).wait()
        near_gather(slot).start()

    def gathered_near(k, slot):
        near_gather(slot).wait()
        leap = k // LOCAL
        rung = core * LOCAL + slot
        eps = step_ref[rung]
        edge = jnp.logical_or(leap == 0, leap == LEAPS)
        kick = jnp.where(edge, 0.5 * eps, eps)
        theta = th_ref[rung]
        force = temp_ref[rung] * gfull[slot].astype(F32) + theta
        moment = mo_ref[rung] - kick * force
        mo_ref[rung] = moment

        @pl.when(leap < LEAPS)
        def _():
            th_ref[rung] = theta + eps * moment

        @pl.when(leap == LEAPS - 1)
        def _():
            result_to_core(th_ref, 0, slot).start()

        @pl.when(leap == LEAPS)
        def _():
            result_to_core(mo_ref, 1, slot).start()

    def turn(k, carry):
        slot = lax.rem(k, LOCAL)
        before = 1 - slot

        @pl.when(k < items)
        def _():
            evaluate(slot, 0)

        @pl.when(k >= 1)
        def _():
            reduced_line(k - 1, before)

        @pl.when(k < items)
        def _():
            evaluate(slot, 1)
            send_near(k, slot)

        @pl.when(k >= 1)
        def _():
            gathered_line(before)

        @pl.when(k < items)
        def _():
            reduced_near(k, slot)

        @pl.when(k >= 1)
        def _():
            gathered_near(k - 1, before)

        return carry

    lax.fori_loop(0, items + 1, turn, 0)
    for s in range(LOCAL):
        result_to_core(th_ref, 0, s).wait()
        result_to_core(mo_ref, 1, s).wait()
    loss_to_core().wait()


def swap_kernel(total_rows, rungs, th_ref, mo_ref, loss_ref, accept_ref, pos_out, mom_out, mean_out):
    order = [jnp.int32(r) for r in range(rungs)]
    for k in range(rungs - 1):
        taken = accept_ref[k] == 1
        lower, upper = order[k], order[k + 1]
        order[k] = jnp.where(taken, upper, lower)
        order[k + 1] = jnp.where(taken, lower, upper)
    means = []
    for r in range(rungs):
        row = (r // LOCAL) * 8 + r % LOCAL
        means.append(jnp.sum(loss_ref[row : row + 1, :]) / total_rows)
    for r in range(rungs):
        pos_out[r] = th_ref[order[r]].T
        mom_out[r] = mo_ref[order[r]].T
        mean = means[0]
        for s in range(1, rungs):
            mean = jnp.where(order[r] == s, means[s], mean)
        mean_out[r] = mean


def local(
    features, treatment, outcome, head, positions, momenta, inverse_temps, step_sizes, accept
):
    rungs, width, hidden = positions.shape
    rows = features.shape[0]
    devices = lax.axis_size("dp")
    line = devices // 4
    vmem = pl.BlockSpec(memory_space=pltpu.VMEM)
    smem = pl.BlockSpec(memory_space=pltpu.SMEM)
    anywhere = pl.BlockSpec(memory_space=pl.ANY)
    half = hidden // 2
    shard = half // line
    block = 256
    dma = pltpu.SemaphoreType.DMA
    theta, moment, loss = pl.pallas_call(
        functools.partial(chain_kernel, line, block),
        out_shape=(
            jax.ShapeDtypeStruct((rungs, hidden, width), F32),
            jax.ShapeDtypeStruct((rungs, hidden, width), F32),
            jax.ShapeDtypeStruct((16, 128), F32),
        ),
        in_specs=[vmem, vmem, vmem, vmem, anywhere, anywhere, smem, smem],
        out_specs=(vmem, vmem, vmem),
        scratch_shapes=[
            pltpu.VMEM((2 * LOCAL, width, hidden), F32),
            pltpu.VMEM((2, width, rows), BF16),
            pltpu.VMEM((2, 8, rows), F32),
            pltpu.VMEM((2, hidden, rows), F32),
            pltpu.VMEM((hidden, 128), F32),
            pltpu.VMEM((hidden, 128), F32),
            pltpu.VMEM((hidden, rows), BF16),
            pltpu.VMEM((2, hidden, block), F32),
            pltpu.VMEM((LOCAL, half, width), F32),
            pltpu.VMEM((LOCAL, half, width), F32),
            pltpu.VMEM((LOCAL, shard, width), F32),
            pltpu.VMEM((LOCAL, hidden, width), F32),
            pltpu.VMEM((LOCAL, half, width), BF16),
            pltpu.VMEM((LOCAL, half, width), BF16),
            pltpu.VMEM((LOCAL, half, width), BF16),
            pltpu.VMEM((LOCAL, line - 1, shard, width), BF16),
            pltpu.VMEM((LOCAL, hidden, width), BF16),
            pltpu.VMEM((8, 128), F32),
            pltpu.VMEM((8, 128), F32),
            pltpu.VMEM((line, 8, 128), F32),
            dma((2 * LOCAL,)),
            dma((4,)),
            dma((LOCAL, 2)),
            dma((LOCAL, line - 1, 2)),
            dma((LOCAL, line - 1, 2)),
            dma((LOCAL, 2)),
            dma((2,)),
            dma((line - 1, 2)),
            dma((3, LOCAL, 2)),
        ],
        compiler_params=pltpu.CompilerParams(
            collective_id=0, has_side_effects=True, vmem_limit_bytes=48 * 1024 * 1024
        ),
    )(
        features,
        treatment.reshape(1, rows),
        outcome.reshape(1, rows),
        head,
        positions,
        momenta,
        inverse_temps,
        step_sizes,
    )
    return pl.pallas_call(
        functools.partial(swap_kernel, float(rows * devices), rungs),
        out_shape=(
            jax.ShapeDtypeStruct((rungs, width, hidden), F32),
            jax.ShapeDtypeStruct((rungs, width, hidden), F32),
            jax.ShapeDtypeStruct((rungs,), F32),
        ),
        in_specs=[vmem, vmem, vmem, smem],
        out_specs=(vmem, vmem, smem),
        compiler_params=pltpu.CompilerParams(vmem_limit_bytes=32 * 1024 * 1024),
    )(theta, moment, loss, accept)


def solution(mesh):
    placed = (
        P(("groups", "dp"), None),
        P(("groups", "dp")),
        P(("groups", "dp")),
        P(),
        P("groups", None, None),
        P("groups", None, None),
        P("groups"),
        P("groups"),
        P("groups"),
    )
    return jax.shard_map(
        local,
        mesh=mesh,
        in_specs=placed,
        out_specs=(P("groups", None, None), P("groups", None, None), P("groups")),
        check_vma=False,
    )
```

time: 528 us -> 114 us (0.22)
  waiting for transfers between devices: 425 us -> 0 us
  Pallas kernels: 0 us -> 107 us
  blocking collectives: 30.8 us -> 0 us
  matrix products: 24.2 us -> 0 us
  other arithmetic: 17.9 us -> 0 us
  between operations: 14 us -> 0.68 us
  local copies, waits for them, and re-layouts: 14.8 us -> 6.09 us
    psum x5 -> x0, waiting for transfers between devices: 425 us -> none  [summed_whole(): return lax.psum((grad, nll), 'dp')]
    pallas_call x0 -> x2, Pallas kernels: none -> 107 us  [the longest x1 105 us: local(): pl.pallas_call(functools.partial(chain_kernel, line, block), out_shape=(j...]
    psum x1 -> x0, blocking collectives: 30.8 us -> none  [summed_whole(): return lax.psum((grad, nll), 'dp')]
    dot_general x10 -> x0, matrix products: 24.2 us -> none  [the longest x5 14.6 us: evaluate(): jnp.einsum('nf,rnh->rfh', features, delta, preferred_element_type=jnp.flo...]
    add x3 -> x0, other arithmetic: 5.85 us -> none  [the longest x2 5.59 us: local(): theta = theta + eps * moment]
    sub x7 -> x0, other arithmetic: 5.51 us -> none  [the longest x2 5.28 us: local(): moment = moment - 0.5 * eps * force]
  transfers between devices with their start and end apart: 5 -> 0, of which waited for: 5 -> 0; matrix products, arithmetic and copies ran while one was open for 2% -> 0% of each run, Pallas kernels for 0% -> 0%
where the time goes in v1:
time: 114 us
  Pallas kernels  107 us (94%)
  local copies, waits for them, and re-layouts  6.09 us (5%)
    pallas_call x1, Pallas kernels, local(): pl.pallas_call(functools.partial(chain_kernel, line, block), out_shape=(j...  105 us
    unnamed x18, local copies, waits for them, and re-layouts  6.09 us
    pallas_call x1, Pallas kernels, local(): pl.pallas_call(functools.partial(swap_kernel, float(rows * devices), rung...  2.44 us

profile of v1, /device:TPU:0, one launch (start us, length us, event | category | flops | bytes accessed | tf_op | source)
XLA Modules:
  0.0 113.8 jit_solution(10681897559476055774)
XLA Ops:
  0.6 0.0 copy-start.5
  0.6 0.0 copy-start.6
  0.7 0.0 copy-start.7
  0.7 0.7 copy-done.5
  1.3 0.0 copy-done.6
  1.3 0.0 copy-done.7
  1.3 0.0 copy-start
  1.3 1.2 %copy-done = f32[4,128,512]{2,1,0:T(8,128)S(1)} copy-done((f32[4,128,512]{2,1,0:T(8,128)S(1)}, f32[4,128,512]{2,1,0:T(8,128)}, u32[]{:S(2)}) %copy-start) | copy-done | bytes 1048600
  2.5 0.0 copy-start.1
  2.5 1.2 %copy-done.1 = f32[4,128,512]{2,1,0:T(8,128)S(1)} copy-done((f32[4,128,512]{2,1,0:T(8,128)S(1)}, f32[4,128,512]{2,1,0:T(8,128)}, u32[]{:S(2)}) %copy-start.1) | copy-done | bytes 1048600
  3.8 0.0 copy-start.2
  3.8 0.9 copy-done.2
  4.7 0.0 copy-start.3
  4.7 0.7 copy-done.3
  5.4 0.0 copy-start.4
  5.4 0.7 copy-done.4
  6.1 104.6 %shard_map.112 = (f32[4,512,128]{2,1,0:T(8,128)S(1)}, f32[4,512,128]{2,1,0:T(8,128)S(1)}, f32[16,128]{1,0:T(8,128)S(1)}) custom-call(bf16[1024,128]{1,0:T(8,128)(2,1)S(1)} %copy-done.2, s32[1,1024]{1,0:T(1,128)S(1)} %bitcast.2, s32[1,1024]{1,0:T(1,128)S(1)} %bitcast.3, bf16[2,512]{1,0:T(2,128)(2,1)S(1)} %copy-done.5, f32[4,128,512]{2,1,0:T(8,128)S(1)} %copy-done, ...), custom_call_target="tpu_custom_call" | custom-call | tf_op jit(solution)/shard_map/pallas_call | solution.py:386
  110.7 0.0 copy-start.8
  110.7 0.6 copy-done.8
  111.4 2.4 %shard_map.113 = (f32[4,128,512]{2,1,0:T(8,128)}, f32[4,128,512]{2,1,0:T(8,128)}, f32[4]{0:T(128)}) custom-call(f32[4,512,128]{2,1,0:T(8,128)S(1)} %get-tuple-element.6.th_ref, f32[4,512,128]{2,1,0:T(8,128)S(1)} %get-tuple-element.7.mo_ref, f32[16,128]{1,0:T(8,128)S(1)} %get-tuple-element.8.loss_ref, s32[3]{0:T(128)S(1)} %copy-done.8), custom_call_target="tpu_custom_call" | custom-call | tf_op jit(solution)/shard_map/pallas_call | solution.py:439
Async XLA Ops:
  0.6 0.7 copy-start.5
  0.6 0.7 copy-start.6
  0.7 0.7 copy-start.7
  1.3 1.2 %copy-start = (f32[4,128,512]{2,1,0:T(8,128)S(1)}, f32[4,128,512]{2,1,0:T(8,128)}, u32[]{:S(2)}) copy-start(f32[4,128,512]{2,1,0:T(8,128)} %pos_ref.1) | copy-start | bytes 3145732
  2.5 1.2 %copy-start.1 = (f32[4,128,512]{2,1,0:T(8,128)S(1)}, f32[4,128,512]{2,1,0:T(8,128)}, u32[]{:S(2)}) copy-start(f32[4,128,512]{2,1,0:T(8,128)} %mom_ref.1) | copy-start | bytes 3145732
  3.8 0.9 copy-start.2
  4.7 0.7 copy-start.3
  5.4 0.7 copy-start.4
  110.7 0.7 copy-start.8

commit v2 on v1

--- a/solution.py
+++ b/solution.py
@@ -133,11 +133,14 @@
             coef[part, :, span] = base_b[...] + ty[part, 0:1, span] * effect_b[...]
     copy_x.wait()
 
-    def near_reduce(slot):
-        return remote(
-            near_send.at[slot],
-            near_recv.at[slot],
-            (near_sem.at[slot, 0], near_sem.at[slot, 1]),
+    turns = line_peers + [far]
+
+    def near_reduce(slot, d):
+        piece = pl.ds(pl.multiple_of(turns[d] * shard, shard), shard)
+        return remote(
+            near_send.at[slot, piece],
+            near_recv.at[slot, piece],
+            (near_sem.at[slot, d, 0], near_sem.at[slot, d, 1]),
             near_peer,
         )
 
@@ -159,12 +162,13 @@
             device(line_peers[d], near, core),
         )
 
-    def near_gather(slot):
-        mine = pl.ds(pl.multiple_of(near * half, half), half)
+    def near_gather(slot, d):
+        owner = lax.rem(far + line - d, line)
+        mine = pl.ds(pl.multiple_of(near * half + owner * shard, shard), shard)
         return remote(
             gfull.at[slot, mine],
             gfull.at[slot, mine],
-            (anear_sem.at[slot, 0], anear_sem.at[slot, 1]),
+            (anear_sem.at[slot, d, 0], anear_sem.at[slot, d, 1]),
             near_peer,
         )
 
@@ -240,20 +244,27 @@
     def send_near(k, slot):
         other = pl.ds(pl.multiple_of((1 - near) * half, half), half)
         near_send[slot] = rounded(gsum[slot, other], near_left, slot, k)
-        near_reduce(slot).start()
+        for d in range(line):
+            near_reduce(slot, d).start()
 
         @pl.when(k == items - 1)
         def _():
             loss_to_near().start()
 
     def reduced_near(k, slot):
-        near_reduce(slot).wait()
-        mine = pl.ds(pl.multiple_of(near * half, half), half)
-        summed = gsum[slot, mine] + near_recv[slot].astype(F32)
-        gsum[slot, mine] = summed
-        line_send[slot] = rounded(summed, line_left, slot, k)
-        for d in range(line - 1):
-            line_reduce(slot, d).start()
+        for d in range(line):
+            near_reduce(slot, d).wait()
+            piece = pl.ds(pl.multiple_of(turns[d] * shard, shard), shard)
+            mine = pl.ds(pl.multiple_of(near * half + turns[d] * shard, shard), shard)
+            summed = gsum[slot, mine] + near_recv[slot, piece].astype(F32)
+            if d == line - 1:
+                gsum[slot, mine] = summed
+            else:
+                value = summed + carry_weight(k) * line_left[slot, piece]
+                sent = value.astype(BF16)
+                line_left[slot, piece] = value - sent.astype(F32)
+                line_send[slot, piece] = sent
+                line_reduce(slot, d).start()
 
         @pl.when(k == items - 1)
         def _():
@@ -271,6 +282,7 @@
         gfull[slot, mine] = rounded(summed, full_left, slot, k)
         for d in range(line - 1):
             line_gather(slot, d).start()
+        near_gather(slot, 0).start()
 
         @pl.when(k == items - 1)
         def _():
@@ -285,10 +297,11 @@
     def gathered_line(slot):
         for d in range(line - 1):
             line_gather(slot, d).wait()
-        near_gather(slot).start()
+            near_gather(slot, d + 1).start()
 
     def gathered_near(k, slot):
-        near_gather(slot).wait()
+        for d in range(line):
+            near_gather(slot, d).wait()
         leap = k // LOCAL
         rung = core * LOCAL + slot
         eps = step_ref[rung]
@@ -415,10 +428,10 @@
             pltpu.VMEM((line, 8, 128), F32),
             dma((2 * LOCAL,)),
             dma((4,)),
-            dma((LOCAL, 2)),
+            dma((LOCAL, line, 2)),
             dma((LOCAL, line - 1, 2)),
             dma((LOCAL, line - 1, 2)),
-            dma((LOCAL, 2)),
+            dma((LOCAL, line, 2)),
             dma((2,)),
             dma((line - 1, 2)),
             dma((3, LOCAL, 2)),

time: 114 us -> 108 us (0.947)
  Pallas kernels: 107 us -> 101 us
    pallas_call x1, Pallas kernels: 105 us -> 98.9 us  [local(): pl.pallas_call(functools.partial(chain_kernel, line, block), out_shape=(j...]
where the time goes in v2:
time: 108 us
  Pallas kernels  101 us (94%)
  local copies, waits for them, and re-layouts  6.09 us (6%)
    pallas_call x1, Pallas kernels, local(): pl.pallas_call(functools.partial(chain_kernel, line, block), out_shape=(j...  98.9 us
    unnamed x18, local copies, waits for them, and re-layouts  6.09 us
    pallas_call x1, Pallas kernels, local(): pl.pallas_call(functools.partial(swap_kernel, float(rows * devices), rung...  2.44 us

profile of v2, /device:TPU:0, one launch (start us, length us, event | category | flops | bytes accessed | tf_op | source)
XLA Modules:
  0.0 108.1 jit_solution(17666311580388493013)
XLA Ops:
  0.6 0.0 copy-start.5
  0.6 0.0 copy-start.6
  0.7 0.0 copy-start.7
  0.7 0.7 copy-done.5
  1.3 0.0 copy-done.6
  1.3 0.0 copy-done.7
  1.3 0.0 copy-start
  1.3 1.2 %copy-done = f32[4,128,512]{2,1,0:T(8,128)S(1)} copy-done((f32[4,128,512]{2,1,0:T(8,128)S(1)}, f32[4,128,512]{2,1,0:T(8,128)}, u32[]{:S(2)}) %copy-start) | copy-done | bytes 1048600
  2.5 0.0 copy-start.1
  2.5 1.2 %copy-done.1 = f32[4,128,512]{2,1,0:T(8,128)S(1)} copy-done((f32[4,128,512]{2,1,0:T(8,128)S(1)}, f32[4,128,512]{2,1,0:T(8,128)}, u32[]{:S(2)}) %copy-start.1) | copy-done | bytes 1048600
  3.8 0.0 copy-start.2
  3.8 0.9 copy-done.2
  4.7 0.0 copy-start.3
  4.7 0.7 copy-done.3
  5.4 0.0 copy-start.4
  5.4 0.7 copy-done.4
  6.1 98.9 %shard_map.112 = (f32[4,512,128]{2,1,0:T(8,128)S(1)}, f32[4,512,128]{2,1,0:T(8,128)S(1)}, f32[16,128]{1,0:T(8,128)S(1)}) custom-call(bf16[1024,128]{1,0:T(8,128)(2,1)S(1)} %copy-done.2, s32[1,1024]{1,0:T(1,128)S(1)} %bitcast.2, s32[1,1024]{1,0:T(1,128)S(1)} %bitcast.3, bf16[2,512]{1,0:T(2,128)(2,1)S(1)} %copy-done.5, f32[4,128,512]{2,1,0:T(8,128)S(1)} %copy-done, ...), custom_call_target="tpu_custom_call" | custom-call | tf_op jit(solution)/shard_map/pallas_call | solution.py:399
  105.0 0.0 copy-start.8
  105.0 0.6 copy-done.8
  105.7 2.4 %shard_map.113 = (f32[4,128,512]{2,1,0:T(8,128)}, f32[4,128,512]{2,1,0:T(8,128)}, f32[4]{0:T(128)}) custom-call(f32[4,512,128]{2,1,0:T(8,128)S(1)} %get-tuple-element.6.th_ref, f32[4,512,128]{2,1,0:T(8,128)S(1)} %get-tuple-element.7.mo_ref, f32[16,128]{1,0:T(8,128)S(1)} %get-tuple-element.8.loss_ref, s32[3]{0:T(128)S(1)} %copy-done.8), custom_call_target="tpu_custom_call" | custom-call | tf_op jit(solution)/shard_map/pallas_call | solution.py:452
Async XLA Ops:
  0.6 0.7 copy-start.5
  0.6 0.7 copy-start.6
  0.7 0.7 copy-start.7
  1.3 1.2 %copy-start = (f32[4,128,512]{2,1,0:T(8,128)S(1)}, f32[4,128,512]{2,1,0:T(8,128)}, u32[]{:S(2)}) copy-start(f32[4,128,512]{2,1,0:T(8,128)} %pos_ref.1) | copy-start | bytes 3145732
  2.5 1.2 %copy-start.1 = (f32[4,128,512]{2,1,0:T(8,128)S(1)}, f32[4,128,512]{2,1,0:T(8,128)}, u32[]{:S(2)}) copy-start(f32[4,128,512]{2,1,0:T(8,128)} %mom_ref.1) | copy-start | bytes 3145732
  3.8 0.9 copy-start.2
  4.7 0.7 copy-start.3
  5.4 0.7 copy-start.4
  105.0 0.7 copy-start.8
